TPU v7x, 256 devices: a whole 4x4x8 slice. The times are simulated.
256 devices in a mesh: ctx: 32 (over x, y, core), head: 8 (over z).
Axes of the slice: x: 4, y: 4, z: 8, core: 2. Of those that a mesh axis runs over, the one named last changes fastest.
Arguments:
- queries: bfloat16 [4, 32, 8192], P(None, 'ctx', 'head')
- kv_cache: bfloat16 [32, 256, 2, 64, 1024], P(None, 'ctx', None, None, 'head'), may hold values from -6 to 6
- new_kv: bfloat16 [4, 32, 2, 1024], P(None, 'ctx', None, 'head'), may hold values from -6 to 6
- selected: int32 [4, 32, 8, 20], P(None, None, 'head'), may hold values from 0 to 255, as said below
- out_weight: bfloat16 [8192, 8192], P('head', 'ctx'), may hold values from -0.0625 to 0.0625
Outputs:
- mixed: bfloat16 [32, 4, 8192], P('head', None, 'ctx')
Inputs may be any that keep to these rules, and one draw needn't show every extreme that they name: Each list selected[s, b, k] names 20 distinct pages; at most 4 of them lie in one aligned block of pages 8 * i to 8 * i + 8 - 1 (the pages of one index of ctx), and exactly 4 in some such block of every list.
All inputs are finite; a program needn't handle non-finite values.
Results may differ from a plain program's by a relative error of at most 0.022.
Values may be sent and summed in bfloat16 or wider, within the bound.
A program may use at most 128 MiB of HBM per device.

v0:
```python
import jax
import jax.numpy as jnp
from jax import lax
from jax.sharding import PartitionSpec as P

HQ = 64
KVH = 8
HD = 128
PAGE = 64


NEG = -1e30


def merged(part, axis, combine):
    gathered = jax.tree.map(lambda a: lax.all_gather(a, axis), part)

    def take(source):
        return jax.tree.map(lambda a: lax.dynamic_index_in_dim(a, source, 0, False), gathered)

    return lax.fori_loop(
        1, lax.axis_size(axis), lambda source, state: combine(state, take(source)), take(0)
    )


def combine(former, latter):
    top_one, total_one, sum_one = former
    top_two, total_two, sum_two = latter
    top_both = jnp.maximum(top_one, top_two)
    factor_one = jnp.exp(top_one - top_both)
    factor_two = jnp.exp(top_two - top_both)
    return (
        top_both,
        total_one * factor_one + total_two * factor_two,
        sum_one * factor_one[..., None] + sum_two * factor_two[..., None],
    )


def partial_of(scores, allowed, values, form):
    masked = jnp.where(allowed, scores, NEG)
    top_score = jnp.max(masked, axis=-1)
    expo = jnp.where(allowed, jnp.exp(masked - top_score[..., None]), 0.0)
    total = jnp.sum(expo, axis=-1)
    weighted = jnp.einsum(
        form, expo.astype(jnp.bfloat16), values, preferred_element_type=jnp.float32
    )
    return (top_score, total, weighted)


def local(queries, kv_cache, new_kv, selected, out_weight):
    steps, own_rows, width = queries.shape
    heads_kv = kv_cache.shape[4] // HD
    groups = HQ // KVH
    pages_dev = kv_cache.shape[1]
    scale = HD ** (-0.5)
    everyone = lax.all_gather(queries, "ctx", axis=1, tiled=True)
    batch = everyone.shape[1]
    q_heads = everyone.reshape(steps, batch, heads_kv, groups, HD)
    first_page = lax.axis_index("ctx") * pages_dev
    keys = kv_cache[:, :, 0].reshape(batch, pages_dev * PAGE, heads_kv, HD)
    values = kv_cache[:, :, 1].reshape(batch, pages_dev * PAGE, heads_kv, HD)
    scores = (
        jnp.einsum("sbkgd,btkd->sbkgt", q_heads, keys, preferred_element_type=jnp.float32) * scale
    )
    numbers = first_page + jnp.arange(pages_dev)
    chosen = jnp.any(selected[..., None] == numbers, axis=3)
    allowed = jnp.repeat(chosen, PAGE, axis=3)[:, :, :, None, :]
    partial_value = partial_of(scores, allowed, values, "sbkgt,btkd->sbkgd")
    own_q = queries.reshape(steps, own_rows, heads_kv, groups, HD)
    new_keys = new_kv[:, :, 0].reshape(steps, own_rows, heads_kv, HD)
    new_values = new_kv[:, :, 1].reshape(steps, own_rows, heads_kv, HD)
    new_scores = (
        jnp.einsum("sbkgd,rbkd->sbkgr", own_q, new_keys, preferred_element_type=jnp.float32) * scale
    )
    causal = (jnp.arange(steps)[None, :] <= jnp.arange(steps)[:, None])[:, None, None, None, :]
    fresh = partial_of(new_scores, causal, new_values, "sbkgr,rbkd->sbkgd")
    own_start = lax.axis_index("ctx") * own_rows
    mine = tuple(
        (lax.dynamic_slice_in_dim(member, own_start, own_rows, 1) for member in partial_value)
    )
    joined = combine(mine, fresh)
    partial_value = tuple(
        (
            lax.dynamic_update_slice_in_dim(member, part_new, own_start, 1)
            for member, part_new in zip(partial_value, joined)
        )
    )
    top_score, total, weighted = merged(partial_value, "ctx", combine)
    attention = (weighted / total[..., None]).astype(jnp.bfloat16).reshape(steps, batch, width)
    by_sequence = jnp.transpose(attention, (1, 0, 2))
    return lax.psum_scatter(
        jnp.einsum(
            "bsf,fd->bsd", by_sequence, out_weight, preferred_element_type=jnp.float32
        ).astype(jnp.bfloat16),
        "head",
        scatter_dimension=0,
        tiled=True,
    )


def solution(mesh):
    return jax.shard_map(
        local,
        mesh=mesh,
        in_specs=(
            P(None, "ctx", "head"),
            P(None, "ctx", None, None, "head"),
            P(None, "ctx", None, "head"),
            P(None, None, "head", None),
            P("head", "ctx"),
        ),
        out_specs=P("head", None, "ctx"),
        check_vma=False,
    )
```

profile of v0, /device:TPU:2, one launch (start us, length us, event | category | flops | bytes accessed | tf_op | source)
XLA Modules:
  0.0 262.1 jit_solution(3239594974096557501)
XLA Ops:
  6.5 0.8 copy.119
  8.1 7.4 %fusion.39 = (bf16[32,8,1,64,128]{4,3,2,1,0:T(8,128)(2,1)}, bf16[32,8,1,64,128]{4,3,2,1,0:T(8,128)(2,1)}) fusion(bf16[32,8,2,64,128]{4,3,2,1,0:T(8,128)(2,1)} %param.8), kind=kLoop, calls=%fused_computation.70 | loop fusion | bytes 16777216 | tf_op jit(solution)/shard_map/slice | solution.py:61
  15.5 24.8 %all_gather.23 = bf16[4,32,1024]{2,0,1:T(4,128)(2,1)S(1)} all-gather(bf16[4,1,1024]{2,0,1:T(4,128)(2,1)S(1)} %copy-done.3), channel_id=1, replica_groups=mesh['ctx'=32,'head'=8] {'ctx'}, dimensions={1}, use_global_device_ids=true | all-gather | bytes 270336 | tf_op jit(solution)/shard_map/all_gather | solution.py:56
  40.7 3.9 %fusion.5 = (f32[4,32,8]{2,0,1:T(4,128)S(1)}, f32[32,512,4,8]{1,3,2,0:T(8,128)S(1)}) fusion(pred[4,32,512]{2,0,1:T(4,128)(4,1)S(1)} %broadcast_in_dim.60, bf16[32,512,128,1]{2,1,3,0:T(8,128)(2,1)} %bitcast.207, bf16[4,32,8,128]{3,2,0,1:T(8,128)(2,1)S(1)} %reshape.210), kind=kOutput, calls=%fused_computation.12 | convolution fusion | flops 135789568 | bytes 6623232 | tf_op jit(solution)/shard_map/sbkgd,btkd->sbkgt/dot_general | solution.py:63
  44.6 0.9 fusion.13
  45.6 0.8 copy-done.2
  46.4 0.9 fusion.11
  47.3 0.8 copy.81
  48.2 1.0 fusion.7
  49.4 23.3 %all_gather.25 = f32[32,4,32,1,8]{2,4,3,1,0:T(8,128)S(1)} all-gather(f32[1,4,32,1,8]{2,4,3,1,0:T(8,128)S(1)} %copy.72), channel_id=1, replica_groups=mesh['ctx'=32,'head'=8] {'ctx'}, dimensions={0}, use_global_device_ids=true | all-gather | bytes 135168 | tf_op jit(solution)/shard_map/all_gather | solution.py:16
  72.7 23.7 %all_gather.27 = f32[32,4,32,1,8]{2,4,3,1,0:T(8,128)S(1)} all-gather(f32[1,4,32,1,8]{2,4,3,1,0:T(8,128)S(1)} %copy.77), channel_id=1, replica_groups=mesh['ctx'=32,'head'=8] {'ctx'}, dimensions={0}, use_global_device_ids=true | all-gather | bytes 135168 | tf_op jit(solution)/shard_map/all_gather | solution.py:16
  96.5 31.5 %all-gather.2.cloned.1.call-done = f32[32,4,32,1,8,128]{5,4,3,2,1,0:T(8,128)} async-done(((f32[1,4,32,1,8,128]{5,4,3,2,1,0:T(8,128)}), f32[32,4,32,1,8,128]{5,4,3,2,1,0:T(8,128)}) %all-gather.2.cloned.1.call-update) | async-done | bytes 16777232 | tf_op jit(solution)/shard_map/all_gather | solution.py:16
  128.0 1.1 slice_bitcast_fusion
  129.0 52.4 %while.19 = (s32[]{:T(128)}, f32[4,32,1,8]{1,3,2,0:T(8,128)S(1)}, f32[4,32,1,8]{1,3,2,0:T(8,128)S(1)}, f32[4,32,1,8,128]{4,3,2,1,0:T(8,128)S(1)}, f32[32,4,32,1,...) while((s32[]{:T(128)}, f32[4,32,1,8]{1,3,2,0:T(8,128)S(1)}, ...), condition=%wide.region_6.7_spmd, body=%wide.region_5.6_spmd.sunk | while | flops 400389 | bytes 1650843 | solution.py:21
  129.3 1.4 fusion.49
  131.0 1.4 fusion.49
  132.7 1.4 fusion.49
  134.4 1.4 fusion.49
  136.0 1.4 fusion.49
  137.7 1.4 fusion.49
  139.4 1.4 fusion.49
  141.1 1.4 fusion.49
  142.8 1.4 fusion.49
  144.5 1.4 fusion.49
  146.2 1.4 fusion.49
  147.9 1.4 fusion.49
  149.6 1.4 fusion.49
  151.3 1.4 fusion.49
  153.0 1.4 fusion.49
  154.6 1.4 fusion.49
  156.3 1.4 fusion.49
  158.0 1.4 fusion.49
  159.7 1.4 fusion.49
  161.4 1.4 fusion.49
  163.1 1.4 fusion.49
  164.8 1.4 fusion.49
  166.5 1.4 fusion.49
  168.2 1.4 fusion.49
  169.9 1.4 fusion.49
  171.6 1.4 fusion.49
  173.2 1.4 fusion.49
  174.9 1.4 fusion.49
  176.6 1.4 fusion.49
  178.3 1.4 fusion.49
  180.0 1.4 fusion.49
  181.9 0.9 convolution_convert_fusion
  184.1 69.8 %all-reduce.3.cloned.1.call-done = bf16[32,4,256]{2,0,1:T(8,128)(2,1)} async-done(((bf16[32,4,256]{2,0,1:T(8,128)(2,1)}), bf16[32,4,256]{2,0,1:T(8,128)(2,1)}) %all-reduce.3.cloned.1.call-update) | async-done | bytes 65552
  253.9 0.7 constant_dynamic-slice_fusion.1
  (196 shorter events, 9.0 us)
Async XLA Ops:
  6.5 175.4 %copy-start = (bf16[1024,256]{1,0:T(8,128)(2,1)S(1)}, bf16[1024,256]{1,0:T(8,128)(2,1)}, u32[]{:S(2)}) copy-start(bf16[1024,256]{1,0:T(8,128)(2,1)} %param.11) | copy-start | bytes 1572868
  6.5 121.4 %all-gather.2.cloned.1.call-start = ((), (), s32[]{:S(2)}) async-start(), calls=%async_computation | async-start | bytes 17301504 | tf_op jit(solution)/shard_map/all_gather | solution.py:16
  8.1 7.4 %copy-start.3 = (bf16[4,1,1024]{2,0,1:T(4,128)(2,1)S(1)}, bf16[4,1,1024]{2,0,1:T(4,128)(2,1)}, u32[]{:S(2)}) copy-start(bf16[4,1,1024]{2,0,1:T(4,128)(2,1)} %param.7) | copy-start | bytes 24580
  8.1 32.3 %copy-start.4 = (bf16[4,1,2,128]{3,2,1,0:T(2,128)(2,1)S(1)}, bf16[4,1,2,128]{3,2,1,0:T(2,128)(2,1)}, u32[]{:S(2)}) copy-start(bf16[4,1,2,128]{3,2,1,0:T(2,128)(2,1)} %param.9) | copy-start | bytes 6148
  40.7 3.9 %copy-start.1 = (bf16[32,8,1,64,128]{4,3,2,1,0:T(8,128)(2,1)S(1)}, bf16[32,8,1,64,128]{4,3,2,1,0:T(8,128)(2,1)}, u32[]{:S(2)}) copy-start(bf16[32,8,1,64,128]{4,3,2,1,0:T(8,128)(2,1)} %get-tuple-element.230) | copy-start | bytes 12582916
  45.6 0.8 copy-start.2
  48.2 205.7 %all-reduce.3.cloned.1.call-start = ((), (), s32[]{:S(2)}) async-start(), calls=%async_computation.1 | async-start | bytes 131072
  181.5 1.3 copy-start.5
Sparse Core Ops, SparseCore 0:
  48.3 79.5 all-gather.1
  182.9 70.9 all-reduce.2
where the time goes:
time: 264 us; the launch traced here: 262 us
  waiting for transfers between devices  101 us (38%)
  blocking collectives  71.8 us (27%)
  other arithmetic  47.7 us (18%)
  local copies, waits for them, and re-layouts  18.7 us (7%)
  between operations  14.3 us (5%)
  matrix products  6.71 us (3%)
    unnamed x3, waiting for transfers between devices  69.9 us
    all_gather x2, blocking collectives, merged(): gathered = jax.tree.map(lambda a: lax.all_gather(a, axis), part)  47 us
    add x31, other arithmetic, combine(): sum_one * factor_one[..., None] + sum_two * factor_two[..., None]  44.9 us
    all_gather x1, waiting for transfers between devices, merged(): gathered = jax.tree.map(lambda a: lax.all_gather(a, axis), part)  31.5 us
    all_gather x1, blocking collectives, local(): everyone = lax.all_gather(queries, 'ctx', axis=1, tiled=True)  24.8 us
    slice x1, local copies, waits for them, and re-layouts, local(): values = kv_cache[:, :, 1].reshape(batch, pages_dev * PAGE, heads_kv, HD)  7.37 us
  transfers between devices with their start and end apart: 2, of which 2 were waited for; matrix products, arithmetic and copies ran while one was open for 1% of the time, Pallas kernels for 0%

commit v1 on v0

v1 whole, which is shorter than its diff:
```python
import functools
import math

import jax
import jax.numpy as jnp
from jax import lax
from jax.experimental import pallas as pl
from jax.experimental.pallas import tpu as pltpu
from jax.sharding import PartitionSpec as P

HQ = 64
KVH = 8
HD = 128
PAGE = 64
GROUPS = HQ // KVH

NEG = -1e30
EXPONENT = HD ** (-0.5) * math.log2(math.e)
BF16 = jnp.bfloat16
F32 = jnp.float32
MESH = pl.DeviceIdType.MESH


def grid_of(size):
    return {32: (4, 4, 2), 8: (2, 2, 2), 4: (2, 1, 2)}[size]


def shifted(me, k, size):
    nx, ny, nc = grid_of(size)
    x, y, c = me // (ny * nc), (me // nc) % ny, me % nc
    dx, dy, dc = k // (ny * nc), (k // nc) % ny, k % nc
    return (((x + dx) % nx) * ny + (y + dy) % ny) * nc + (c + dc) % nc


def softmax_part(scores, values):
    top = jnp.max(scores, axis=-1, keepdims=True)
    expo = jnp.exp2((scores - top) * EXPONENT)
    total = jnp.sum(expo, axis=-1, keepdims=True)
    weighted = jnp.dot(expo.astype(BF16), values, preferred_element_type=F32)
    return weighted * (1.0 / total), top * EXPONENT + jnp.log2(total)


def packed(normed, logs):
    lane = lax.broadcasted_iota(jnp.int32, (8, HD), 1)
    stats = jnp.zeros((8, HD), F32)
    for v in range(normed.shape[0] // 8):
        stats = jnp.where(lane == v, logs[8 * v : 8 * v + 8], stats)
    high = stats.astype(BF16).astype(F32)
    return jnp.concatenate([normed, high, stats - high], axis=0).astype(BF16)


def kernel(
    q_hbm,
    kv_hbm,
    new_hbm,
    sel_hbm,
    w_hbm,
    out_ref,
    q_in,
    new_in,
    sel_in,
    kv,
    w,
    rows32,
    q_all,
    bias,
    part_out,
    part_in,
    att_all,
    att32,
    mix_out,
    mix_in,
    small_sem,
    kv_sem,
    w_sem,
    q_send,
    q_recv,
    part_send,
    part_recv,
    att_send,
    att_recv,
    mix_send,
    mix_recv,
    *,
    n_ctx,
    n_head,
    group,
):
    steps = q_in.shape[0]
    pages = kv.shape[1]
    tokens = pages * PAGE
    rows = steps * GROUPS
    me = lax.axis_index("ctx")
    my_head = lax.axis_index("head")

    def owner(k):
        return shifted(me, k, n_ctx)

    q_copy = pltpu.make_async_copy(q_hbm, q_in, small_sem.at[0])
    sel_copy = pltpu.make_async_copy(sel_hbm, sel_in, small_sem.at[1])
    new_copy = pltpu.make_async_copy(new_hbm, new_in, small_sem.at[2])
    w_copy = pltpu.make_async_copy(w_hbm, w, w_sem)
    q_copy.start()
    sel_copy.start()
    new_copy.start()

    barrier = pltpu.get_barrier_semaphore()

    @pl.loop(1, n_ctx)
    def _(k):
        pl.semaphore_signal(barrier, inc=1, device_id={"ctx": owner(k)}, device_id_type=MESH)

    @pl.loop(1, n_head)
    def _(k):
        pl.semaphore_signal(
            barrier, inc=1, device_id={"head": (my_head + k) % n_head}, device_id_type=MESH
        )

    def kv_copy(k):
        b = owner(k)
        return pltpu.make_async_copy(kv_hbm.at[b], kv.at[b], kv_sem.at[k])

    @pl.loop(0, n_ctx)
    def _(k):
        kv_copy(k).start()

    w_copy.start()

    q_copy.wait()
    for g in range(GROUPS):
        rows32[g * steps : (g + 1) * steps, :] = q_in[:, g * HD : (g + 1) * HD].astype(F32)
    q_all[me] = rows32[...].astype(BF16)

    pl.semaphore_wait(barrier, n_ctx - 1 + n_head - 1)

    @pl.loop(1, n_ctx)
    def _(k):
        pltpu.make_async_remote_copy(
            src_ref=q_all.at[me],
            dst_ref=q_all.at[me],
            send_sem=q_send,
            recv_sem=q_recv.at[me],
            device_id={"ctx": owner(k)},
            device_id_type=MESH,
        ).start()

    sel_copy.wait()
    number = lax.broadcasted_iota(jnp.int32, (pages, n_ctx), 0) + me * pages
    from_b = lax.broadcasted_iota(jnp.int32, (n_ctx, n_ctx * 8), 0)
    to_lane = lax.broadcasted_iota(jnp.int32, (n_ctx, n_ctx * 8), 1)
    chosen = jnp.zeros((pages, n_ctx * 8), F32)
    for s in range(steps):
        hit = jnp.zeros((pages, n_ctx), F32)
        for j in range(sel_in.shape[1]):
            hit = jnp.where(sel_in[s, j] == number, 1.0, hit)
        spread = jnp.where(((to_lane >> 3) == from_b) & ((to_lane & 3) == s), 1.0, 0.0)
        chosen += jnp.dot(hit.astype(BF16), spread.astype(BF16), preferred_element_type=F32)
    page = lax.broadcasted_iota(jnp.int32, (pages, tokens), 0)
    token = lax.broadcasted_iota(jnp.int32, (pages, tokens), 1)
    expand = jnp.where((token >> 6) == page, 1.0, 0.0).astype(BF16)
    count = lax.dot_general(
        chosen.astype(BF16), expand, (((0,), (0,)), ((), ())), preferred_element_type=F32
    )
    bias[...] = ((count - 1.0) * -NEG).reshape(bias.shape)

    new_copy.wait()
    new_keys = jnp.concatenate(
        [new_in[:, 0].astype(F32), jnp.zeros((HD - steps, HD), F32)], axis=0
    ).astype(BF16)
    new_values = jnp.concatenate(
        [new_in[:, 1].astype(F32), jnp.zeros((HD - steps, HD), F32)], axis=0
    ).astype(BF16)
    fresh = lax.dot_general(
        q_all[me], new_keys, (((1,), (1,)), ((), ())), preferred_element_type=F32
    )
    step_of = lax.broadcasted_iota(jnp.int32, (rows, HD), 0) & (steps - 1)
    place = lax.broadcasted_iota(jnp.int32, (rows, HD), 1)
    fresh = jnp.where(place <= step_of, fresh, NEG)
    part_in[n_ctx] = packed(*softmax_part(fresh, new_values))

    @pl.loop(0, n_ctx // group)
    def _(turn):
        for u in range(group):
            k = turn * group + u
            kv_copy(k).wait()

            def wait_query():
                b = owner(k)
                pltpu.make_async_copy(q_all.at[b], q_all.at[b], q_recv.at[b]).wait()

            if u == 0:
                pl.when(turn > 0)(wait_query)
            else:
                wait_query()
        results = []
        for u in range(group):
            b = owner(turn * group + u)
            keys = kv[b, :, 0].reshape(tokens, HD)
            scores = lax.dot_general(
                q_all[b], keys, (((1,), (1,)), ((), ())), preferred_element_type=F32
            )
            scores = (scores.reshape(rows // 8, 8, tokens) + bias[b][None]).reshape(rows, tokens)
            values = kv[b, :, 1].reshape(tokens, HD)
            results.append(packed(*softmax_part(scores, values)))
        for u in range(group):
            part_out[turn * group + u] = results[u]
        for u in range(group):
            k = turn * group + u

            def send():
                pltpu.make_async_remote_copy(
                    src_ref=part_out.at[k],
                    dst_ref=part_in.at[me],
                    send_sem=part_send,
                    recv_sem=part_recv,
                    device_id={"ctx": owner(k)},
                    device_id_type=MESH,
                ).start()

            if u == 0:
                pl.when(turn > 0)(send)
            else:
                send()

    part_in[me] = part_out[0]

    others = pl.ds(0, n_ctx - 1)
    pltpu.make_async_copy(part_in.at[others], part_in.at[others], part_recv).wait()
    logs = [part_in[i, rows : rows + 16, :].astype(F32) for i in range(n_ctx + 1)]
    logs = [pair[0:8] + pair[8:16] for pair in logs]
    top = functools.reduce(jnp.maximum, logs)
    shares = [jnp.exp2(log - top) for log in logs]
    total = functools.reduce(jnp.add, shares)
    inverse = 1.0 / total
    joined = [jnp.zeros((8, HD), F32) for _ in range(rows // 8)]
    for i in range(n_ctx + 1):
        share = shares[i] * inverse
        part = part_in[i, 0:rows, :].astype(F32)
        for v in range(rows // 8):
            joined[v] += part[8 * v : 8 * v + 8] * share[:, v : v + 1]
    rows32[...] = jnp.concatenate(joined, axis=0)
    attention = jnp.concatenate(
        [rows32[pl.ds(s, GROUPS, stride=steps), :] for s in range(steps)], axis=0
    )
    att_all[me] = attention.astype(BF16)

    @pl.loop(1, n_ctx)
    def _(k):
        pltpu.make_async_remote_copy(
            src_ref=att_all.at[me],
            dst_ref=att_all.at[me],
            send_sem=att_send,
            recv_sem=att_recv,
            device_id={"ctx": owner(k)},
            device_id_type=MESH,
        ).start()

    w_copy.wait()
    pltpu.make_async_copy(att_all.at[others], att_all.at[others], att_recv).wait()

    att32[...] = att_all[...].astype(F32).reshape(att32.shape)
    flat = jnp.concatenate(
        [att32[pl.ds(g, n_ctx * steps, stride=GROUPS), :].astype(BF16) for g in range(GROUPS)],
        axis=1,
    )
    mixed = jnp.dot(flat, w[...], preferred_element_type=F32)
    mix_out[...] = mixed.astype(BF16).reshape(mix_out.shape)

    @pl.loop(1, n_head)
    def _(k):
        to = (my_head + k) % n_head
        pltpu.make_async_remote_copy(
            src_ref=mix_out.at[to],
            dst_ref=mix_in.at[my_head],
            send_sem=mix_send,
            recv_sem=mix_recv,
            device_id={"head": to},
            device_id_type=MESH,
        ).start()

    mix_in[my_head] = mix_out[my_head]
    other_heads = pl.ds(0, n_head - 1)
    pltpu.make_async_copy(mix_in.at[other_heads], mix_in.at[other_heads], mix_recv).wait()
    out_ref[...] = jnp.sum(mix_in[...].astype(F32), axis=0).astype(BF16)

    pltpu.make_async_copy(q_all.at[others], q_all.at[others], q_send).wait()
    pltpu.make_async_copy(part_out.at[others], part_out.at[others], part_send).wait()
    pltpu.make_async_copy(att_all.at[others], att_all.at[others], att_send).wait()
    pltpu.make_async_copy(mix_out.at[other_heads], mix_out.at[other_heads], mix_send).wait()


def local(queries, kv_cache, new_kv, selected, out_weight, *, n_ctx, n_head, group):
    steps, _, width = queries.shape
    batch, pages = kv_cache.shape[:2]
    rows = steps * GROUPS
    columns = out_weight.shape[1]
    own = batch // n_head * steps
    dma = pltpu.SemaphoreType.DMA
    any_space = pl.BlockSpec(memory_space=pl.ANY)
    sel = jnp.transpose(selected, (0, 3, 2, 1))
    result = pl.pallas_call(
        functools.partial(kernel, n_ctx=n_ctx, n_head=n_head, group=group),
        out_shape=jax.ShapeDtypeStruct((own, columns), BF16),
        in_specs=[any_space] * 5,
        out_specs=pl.BlockSpec(memory_space=pltpu.VMEM),
        scratch_shapes=[
            pltpu.VMEM((steps, width), BF16),
            pltpu.VMEM((steps, 2, HD), BF16),
            pltpu.VMEM(sel.shape, jnp.int32),
            pltpu.VMEM(kv_cache.shape, BF16),
            pltpu.VMEM(out_weight.shape, BF16),
            pltpu.VMEM((rows, HD), F32),
            pltpu.VMEM((batch, rows, HD), BF16),
            pltpu.VMEM((batch, 8, pages * PAGE), F32),
            pltpu.VMEM((n_ctx, rows + 16, HD), BF16),
            pltpu.VMEM((n_ctx + 1, rows + 16, HD), BF16),
            pltpu.VMEM((batch, rows, HD), BF16),
            pltpu.VMEM((batch * rows, HD), F32),
            pltpu.VMEM((n_head, own, columns), BF16),
            pltpu.VMEM((n_head, own, columns), BF16),
            dma((3,)),
            dma((n_ctx,)),
            dma,
            dma,
            dma((n_ctx,)),
            dma,
            dma,
            dma,
            dma,
            dma,
            dma,
        ],
        compiler_params=pltpu.CompilerParams(
            collective_id=0, has_side_effects=True, vmem_limit_bytes=56 * 1024 * 1024
        ),
    )(
        queries.reshape(steps, width),
        kv_cache,
        new_kv.reshape(steps, 2, HD),
        sel,
        out_weight,
    )
    return result.reshape(batch // n_head, steps, columns)


def solution(mesh):
    n_ctx, n_head = mesh.shape["ctx"], mesh.shape["head"]
    return jax.shard_map(
        functools.partial(local, n_ctx=n_ctx, n_head=n_head, group=4),
        mesh=mesh,
        in_specs=(
            P(None, "ctx", "head"),
            P(None, "ctx", None, None, "head"),
            P(None, "ctx", None, "head"),
            P(None, None, "head", None),
            P("head", "ctx"),
        ),
        out_specs=P("head", None, "ctx"),
        check_vma=False,
    )
```

time: 264 us -> 43.5 us (0.16)
  the two profiles are of different devices: /device:TPU:2 before, /device:TPU:1 now
where the time goes in v1:
time: 43.5 us; the launch traced here: 43.3 us
  Pallas kernels  42 us (97%)
  local copies, waits for them, and re-layouts  1.3 us (3%)
    pallas_call x1, Pallas kernels, local(): pl.pallas_call(functools.partial(kernel, n_ctx=n_ctx, n_head=n_head, grou...  42 us
    reshape x1, local copies, waits for them, and re-layouts, local(): return result.reshape(batch // n_head, steps, columns)  1.3 us

profile of v1, /device:TPU:1, one launch (start us, length us, event | category | flops | bytes accessed | tf_op | source)
XLA Modules:
  0.0 43.3 jit_solution(1397912766667474259)
XLA Ops:
  0.0 42.0 %shard_map.55 = bf16[16,256]{1,0:T(8,128)(2,1)} custom-call(bf16[4,1024]{1,0:T(4,128)(2,1)} %bitcast.4, bf16[32,8,2,64,128]{4,3,2,1,0:T(8,128)(2,1)} %kv_hbm.1, bf16[4,2,128]{2,1,0:T(2,128)(2,1)} %bitcast.5, s32[4,20,1,32]{3,2,1,0:T(1,128)} %bitcast.3, bf16[1024,256]{1,0:T(8,128)(2,1)} %w_hbm.1), custom_call_target="tpu_custom_call" | custom-call | tf_op jit(solution)/shard_map/pallas_call | solution.py:301
  42.0 1.3 %reshape.11 = bf16[4,4,256]{2,1,0:T(4,128)(2,1)} reshape(bf16[16,256]{1,0:T(8,128)(2,1)} %shard_map.55) | data formatting | bytes 16384 | tf_op jit(solution)/shard_map/reshape | solution.py:343

commit v2 on v1

v2 whole, which is shorter than its diff:
```python
import functools
import math

import jax
import jax.numpy as jnp
from jax import lax
from jax.experimental import pallas as pl
from jax.experimental.pallas import tpu as pltpu
from jax.sharding import PartitionSpec as P

HQ = 64
KVH = 8
HD = 128
PAGE = 64
GROUPS = HQ // KVH

NEG = -1e30
EXPONENT = HD ** (-0.5) * math.log2(math.e)
BF16 = jnp.bfloat16
F32 = jnp.float32
MESH = pl.DeviceIdType.MESH


def displacements(size):
    sizes = {32: (4, 4, 2), 8: (2, 2, 2), 4: (2, 1, 2)}[size]
    nx, ny, nc = sizes
    every = [(x, y, c) for x in range(nx) for y in range(ny) for c in range(nc)][1:]

    def hops(d):
        return min(d[0], nx - d[0]) + min(d[1], ny - d[1])

    every = sorted(every, key=lambda d: -hops(d))
    parts = [[d for d in every if hops(d) >= 3], [d for d in every if hops(d) == 2], [d for d in every if hops(d) < 2]]
    return sizes, [part for part in parts if part]


def by_distance(size):
    return sorted(range(1, size), key=lambda d: -min(d, size - d))


def softmax_parts(queries, keys, values, masked):
    scores = [
        mask(lax.dot_general(q, k, (((1,), (1,)), ((), ())), preferred_element_type=F32))
        for q, k, mask in zip(queries, keys, masked)
    ]
    tops = [jnp.max(x, axis=-1, keepdims=True) for x in scores]
    expos = [jnp.exp2((x - top) * EXPONENT) for x, top in zip(scores, tops)]
    totals = [jnp.sum(x, axis=-1, keepdims=True) for x in expos]
    sums = [
        jnp.dot(x.astype(BF16), v, preferred_element_type=F32) for x, v in zip(expos, values)
    ]
    return [
        ((x * (1.0 / total)).astype(BF16), as_row(top * EXPONENT + jnp.log2(total)))
        for x, top, total in zip(sums, tops, totals)
    ]


def as_row(column):
    lane = lax.broadcasted_iota(jnp.int32, (8, HD), 1)
    sublane = lax.broadcasted_iota(jnp.int32, (8, HD), 0)
    spread = jnp.zeros((8, HD), F32)
    for v in range(column.shape[0] // 8):
        spread = jnp.where(lane == sublane + 8 * v, column[8 * v : 8 * v + 8], spread)
    return jnp.sum(spread, axis=0, keepdims=True)


def kernel(
    q_hbm,
    kv_hbm,
    new_hbm,
    sel_hbm,
    w_hbm,
    out_ref,
    q_in,
    new_in,
    sel_in,
    kv,
    w,
    rows32,
    q_all,
    bias,
    part_out,
    part_in,
    log_out,
    log_in,
    att_all,
    att32,
    mix_out,
    mix_in,
    small_sem,
    kv_sem,
    w_sem,
    q_send,
    q_recv,
    part_send,
    part_recv,
    log_send,
    log_recv,
    att_send,
    att_recv,
    mix_send,
    mix_recv,
    *,
    n_ctx,
    n_head,
):
    steps = q_in.shape[0]
    pages = kv.shape[1]
    tokens = pages * PAGE
    rows = steps * GROUPS
    me = lax.axis_index("ctx")
    my_head = lax.axis_index("head")

    (nx, ny, nc), parts = displacements(n_ctx)
    others_list = [d for part in parts for d in part]
    x, y, c = me // (ny * nc), (me // nc) & (ny - 1), me & (nc - 1)

    def owner(d):
        return (((x + d[0]) & (nx - 1)) * ny + ((y + d[1]) & (ny - 1))) * nc + ((c + d[2]) & (nc - 1))

    def back(d):
        opposite = ((nx - d[0]) % nx, (ny - d[1]) % ny, (nc - d[2]) % nc)
        return next(i for i, part in enumerate(parts) if opposite in part)

    q_copy = pltpu.make_async_copy(q_hbm, q_in, small_sem.at[0])
    sel_copy = pltpu.make_async_copy(sel_hbm, sel_in, small_sem.at[1])
    new_copy = pltpu.make_async_copy(new_hbm, new_in, small_sem.at[2])
    w_copy = pltpu.make_async_copy(w_hbm, w, w_sem)
    q_copy.start()
    sel_copy.start()
    new_copy.start()

    barrier = pltpu.get_barrier_semaphore()

    for d in others_list:
        pl.semaphore_signal(barrier, inc=1, device_id={"ctx": owner(d)}, device_id_type=MESH)
    for d in by_distance(n_head):
        to = lax.rem(my_head + d, n_head)
        pl.semaphore_signal(barrier, inc=1, device_id={"head": to}, device_id_type=MESH)

    chunk = kv.shape[0] // 4
    for i in range(4):
        part = pl.ds(i * chunk, chunk)
        pltpu.make_async_copy(kv_hbm.at[part], kv.at[part], kv_sem).start()
    w_copy.start()

    q_copy.wait()
    for g in range(GROUPS):
        rows32[g * steps : (g + 1) * steps, :] = q_in[:, g * HD : (g + 1) * HD].astype(F32)
    q_all[me] = rows32[...].astype(BF16)

    pl.semaphore_wait(barrier, n_ctx - 1 + n_head - 1)

    for d in others_list:
        pltpu.make_async_remote_copy(
            src_ref=q_all.at[me],
            dst_ref=q_all.at[me],
            send_sem=q_send,
            recv_sem=q_recv.at[back(d)],
            device_id={"ctx": owner(d)},
            device_id_type=MESH,
        ).start()

    sel_copy.wait()
    number = lax.broadcasted_iota(jnp.int32, (pages, n_ctx), 0) + me * pages
    from_b = lax.broadcasted_iota(jnp.int32, (n_ctx, n_ctx * 8), 0)
    to_lane = lax.broadcasted_iota(jnp.int32, (n_ctx, n_ctx * 8), 1)
    chosen = jnp.zeros((pages, n_ctx * 8), F32)
    for s in range(steps):
        hit = jnp.zeros((pages, n_ctx), F32)
        for j in range(sel_in.shape[1]):
            hit = jnp.where(sel_in[s, j] == number, 1.0, hit)
        spread = jnp.where(((to_lane >> 3) == from_b) & ((to_lane & 3) == s), 1.0, 0.0)
        chosen += jnp.dot(hit.astype(BF16), spread.astype(BF16), preferred_element_type=F32)
    page = lax.broadcasted_iota(jnp.int32, (pages, tokens), 0)
    token = lax.broadcasted_iota(jnp.int32, (pages, tokens), 1)
    expand = jnp.where((token >> 6) == page, 1.0, 0.0).astype(BF16)
    count = lax.dot_general(
        chosen.astype(BF16), expand, (((0,), (0,)), ((), ())), preferred_element_type=F32
    )
    bias[...] = ((count - 1.0) * -NEG).reshape(bias.shape)

    new_copy.wait()
    new_keys = jnp.concatenate(
        [new_in[:, 0].astype(F32), jnp.zeros((HD - steps, HD), F32)], axis=0
    ).astype(BF16)
    new_values = jnp.concatenate(
        [new_in[:, 1].astype(F32), jnp.zeros((HD - steps, HD), F32)], axis=0
    ).astype(BF16)
    step_of = lax.broadcasted_iota(jnp.int32, (rows, HD), 0) & (steps - 1)
    place = lax.broadcasted_iota(jnp.int32, (rows, HD), 1)

    def causal(scores):
        return jnp.where(place <= step_of, scores, NEG)

    def selected_of(b):
        def mask(scores):
            return (scores.reshape(rows // 8, 8, tokens) + bias[b][None]).reshape(rows, tokens)

        return mask

    def keys_of(b):
        return kv[b, :, 0].reshape(tokens, HD)

    def values_of(b):
        return kv[b, :, 1].reshape(tokens, HD)

    pltpu.make_async_copy(kv, kv, kv_sem).wait()
    own = q_all[me]
    (fresh_part, fresh_log), (own_part, own_log) = softmax_parts(
        [own, own], [new_keys, keys_of(me)], [new_values, values_of(me)], [causal, selected_of(me)]
    )
    part_in[n_ctx], log_in[n_ctx] = fresh_part, fresh_log
    part_in[me], log_in[me] = own_part, own_log
    for i in range(n_ctx + 1, log_in.shape[0]):
        log_in[i] = jnp.full((1, HD), NEG, F32)

    done = 0
    for i, part in enumerate(parts):
        block = pl.ds(0, len(part))
        pltpu.make_async_copy(q_all.at[block], q_all.at[block], q_recv.at[i]).wait()
        owners = [owner(d) for d in part]
        results = softmax_parts(
            [q_all[b] for b in owners],
            [keys_of(b) for b in owners],
            [values_of(b) for b in owners],
            [selected_of(b) for b in owners],
        )
        for u, (normed, log) in enumerate(results):
            part_out[done + u], log_out[done + u] = normed, log
        for u, b in enumerate(owners):
            for out, into, send_sem, recv_sem in (
                (log_out, log_in, log_send, log_recv),
                (part_out, part_in, part_send, part_recv),
            ):
                pltpu.make_async_remote_copy(
                    src_ref=out.at[done + u],
                    dst_ref=into.at[me],
                    send_sem=send_sem,
                    recv_sem=recv_sem,
                    device_id={"ctx": b},
                    device_id_type=MESH,
                ).start()
        done += len(part)

    others = pl.ds(0, n_ctx - 1)
    pltpu.make_async_copy(log_in.at[others], log_in.at[others], log_recv).wait()
    logs = log_in[...].reshape(log_in.shape[0], HD)
    shares = jnp.exp2(logs - jnp.max(logs, axis=0, keepdims=True))
    shares = shares * (1.0 / jnp.sum(shares, axis=0, keepdims=True))
    columns = jnp.transpose(shares)
    pltpu.make_async_copy(part_in.at[others], part_in.at[others], part_recv).wait()
    joined = [jnp.zeros((8, HD), F32) for _ in range(rows // 8)]
    for i in range(n_ctx + 1):
        part = part_in[i].astype(F32)
        for v in range(rows // 8):
            joined[v] += part[8 * v : 8 * v + 8] * columns[8 * v : 8 * v + 8, i : i + 1]
    rows32[...] = jnp.concatenate(joined, axis=0)
    attention = jnp.concatenate(
        [rows32[pl.ds(s, GROUPS, stride=steps), :] for s in range(steps)], axis=0
    )
    att_all[me] = attention.astype(BF16)

    for d in others_list:
        pltpu.make_async_remote_copy(
            src_ref=att_all.at[me],
            dst_ref=att_all.at[me],
            send_sem=att_send,
            recv_sem=att_recv,
            device_id={"ctx": owner(d)},
            device_id_type=MESH,
        ).start()

    w_copy.wait()
    pltpu.make_async_copy(att_all.at[others], att_all.at[others], att_recv).wait()

    att32[...] = att_all[...].astype(F32).reshape(att32.shape)
    flat = jnp.concatenate(
        [att32[pl.ds(g, n_ctx * steps, stride=GROUPS), :].astype(BF16) for g in range(GROUPS)],
        axis=1,
    )
    mixed = jnp.dot(flat, w[...], preferred_element_type=F32)
    mix_out[...] = mixed.astype(BF16).reshape(mix_out.shape)

    for d in by_distance(n_head):
        to = lax.rem(my_head + d, n_head)
        pltpu.make_async_remote_copy(
            src_ref=mix_out.at[to],
            dst_ref=mix_in.at[my_head],
            send_sem=mix_send,
            recv_sem=mix_recv,
            device_id={"head": to},
            device_id_type=MESH,
        ).start()

    mix_in[my_head] = mix_out[my_head]
    other_heads = pl.ds(0, n_head - 1)
    pltpu.make_async_copy(mix_in.at[other_heads], mix_in.at[other_heads], mix_recv).wait()
    out_ref[...] = jnp.sum(mix_in[...].astype(F32), axis=0).astype(BF16)

    pltpu.make_async_copy(q_all.at[others], q_all.at[others], q_send).wait()
    pltpu.make_async_copy(part_out, part_out, part_send).wait()
    pltpu.make_async_copy(log_out, log_out, log_send).wait()
    pltpu.make_async_copy(att_all.at[others], att_all.at[others], att_send).wait()
    pltpu.make_async_copy(mix_out.at[other_heads], mix_out.at[other_heads], mix_send).wait()


def local(queries, kv_cache, new_kv, selected, out_weight, *, n_ctx, n_head):
    steps, _, width = queries.shape
    batch, pages = kv_cache.shape[:2]
    rows = steps * GROUPS
    columns = out_weight.shape[1]
    own = batch // n_head * steps
    dma = pltpu.SemaphoreType.DMA
    any_space = pl.BlockSpec(memory_space=pl.ANY)
    sel = jnp.transpose(selected, (0, 3, 2, 1))
    result = pl.pallas_call(
        functools.partial(kernel, n_ctx=n_ctx, n_head=n_head),
        out_shape=jax.ShapeDtypeStruct((own, columns), BF16),
        in_specs=[any_space] * 5,
        out_specs=pl.BlockSpec(memory_space=pltpu.VMEM),
        scratch_shapes=[
            pltpu.VMEM((steps, width), BF16),
            pltpu.VMEM((steps, 2, HD), BF16),
            pltpu.VMEM(sel.shape, jnp.int32),
            pltpu.VMEM(kv_cache.shape, BF16),
            pltpu.VMEM(out_weight.shape, BF16),
            pltpu.VMEM((rows, HD), F32),
            pltpu.VMEM((batch, rows, HD), BF16),
            pltpu.VMEM((batch, 8, pages * PAGE), F32),
            pltpu.VMEM((n_ctx - 1, rows, HD), BF16),
            pltpu.VMEM((n_ctx + 1, rows, HD), BF16),
            pltpu.VMEM((n_ctx - 1, 1, HD), F32),
            pltpu.VMEM((n_ctx + 8, 1, HD), F32),
            pltpu.VMEM((batch, rows, HD), BF16),
            pltpu.VMEM((batch * rows, HD), F32),
            pltpu.VMEM((n_head, own, columns), BF16),
            pltpu.VMEM((n_head, own, columns), BF16),
            dma((3,)),
            dma,
            dma,
            dma,
            dma((3,)),
            dma,
            dma,
            dma,
            dma,
            dma,
            dma,
            dma,
            dma,
        ],
        compiler_params=pltpu.CompilerParams(
            collective_id=0, has_side_effects=True, vmem_limit_bytes=56 * 1024 * 1024
        ),
    )(
        queries.reshape(steps, width),
        kv_cache,
        new_kv.reshape(steps, 2, HD),
        sel,
        out_weight,
    )
    return result.reshape(batch // n_head, steps, columns)


def solution(mesh):
    n_ctx, n_head = mesh.shape["ctx"], mesh.shape["head"]
    return jax.shard_map(
        functools.partial(local, n_ctx=n_ctx, n_head=n_head),
        mesh=mesh,
        in_specs=(
            P(None, "ctx", "head"),
            P(None, "ctx", None, None, "head"),
            P(None, "ctx", None, "head"),
            P(None, None, "head", None),
            P("head", "ctx"),
        ),
        out_specs=P("head", None, "ctx"),
        check_vma=False,
    )
```

time: 43.5 us -> 35.1 us (0.81)
  Pallas kernels: 42 us -> 33.6 us
    pallas_call x1, Pallas kernels: 42 us -> 33.6 us  [local(): pl.pallas_call(functools.partial(kernel, n_ctx=n_ctx, n_head=n_head), out...]
where the time goes in v2:
time: 35.1 us; the launch traced here: 34.9 us
  Pallas kernels  33.6 us (96%)
  local copies, waits for them, and re-layouts  1.3 us (4%)
    pallas_call x1, Pallas kernels, local(): pl.pallas_call(functools.partial(kernel, n_ctx=n_ctx, n_head=n_head), out...  33.6 us
    reshape x1, local copies, waits for them, and re-layouts, local(): return result.reshape(batch // n_head, steps, columns)  1.3 us

profile of v2, /device:TPU:1, one launch (start us, length us, event | category | flops | bytes accessed | tf_op | source)
XLA Modules:
  0.0 34.9 jit_solution(10139859805210469449)
XLA Ops:
  0.0 33.6 %shard_map.55 = bf16[16,256]{1,0:T(8,128)(2,1)} custom-call(bf16[4,1024]{1,0:T(4,128)(2,1)} %bitcast.4, bf16[32,8,2,64,128]{4,3,2,1,0:T(8,128)(2,1)} %kv_hbm.1, bf16[4,2,128]{2,1,0:T(2,128)(2,1)} %bitcast.5, s32[4,20,1,32]{3,2,1,0:T(1,128)} %bitcast.3, bf16[1024,256]{1,0:T(8,128)(2,1)} %w_hbm.1), custom_call_target="tpu_custom_call" | custom-call | tf_op jit(solution)/shard_map/pallas_call | solution.py:317
  33.6 1.3 %reshape.11 = bf16[4,4,256]{2,1,0:T(4,128)(2,1)} reshape(bf16[16,256]{1,0:T(8,128)(2,1)} %shard_map.55) | data formatting | bytes 16384 | tf_op jit(solution)/shard_map/reshape | solution.py:363

commit v3 on v2

v3 whole, which is shorter than its diff:
```python
import functools
import math

import jax
import jax.numpy as jnp
from jax import lax
from jax.experimental import pallas as pl
from jax.experimental.pallas import tpu as pltpu
from jax.sharding import PartitionSpec as P

HQ = 64
KVH = 8
HD = 128
PAGE = 64
GROUPS = HQ // KVH

NEG = -1e30
EXPONENT = HD ** (-0.5) * math.log2(math.e)
BF16 = jnp.bfloat16
F32 = jnp.float32
MESH = pl.DeviceIdType.MESH


def axes_of(size):
    return {32: (4, 4, 2), 8: (2, 2, 2)}[size]


def displacements(size):
    nx, ny, nc = axes_of(size)
    every = [(x, y, c) for x in range(nx) for y in range(ny) for c in range(nc)][1:]
    return sorted(every, key=lambda d: -min(d[0], nx - d[0]) - min(d[1], ny - d[1]))


def half_of(x, y, c, size):
    nx, ny, _ = axes_of(size)
    return c * (nx * ny) + ((x + y) & 1) * (nx * ny // 2) + x * (ny // 2) + (y >> 1)


def log2_of(size):
    return size.bit_length() - 1


def joiner_of(half, size):
    nx, ny, nc = axes_of(size)
    chips = nx * ny
    c, place = half >> log2_of(chips), half & (chips - 1)
    odd, place = place >> log2_of(chips // 2), place & (chips // 2 - 1)
    x = place >> log2_of(ny // 2)
    y = 2 * (place & (ny // 2 - 1)) + ((x + odd) & 1)
    return (x * ny + y) * nc + c


def by_distance(size):
    return sorted(range(1, size), key=lambda d: -min(d, size - d))


def softmax_parts(queries, keys, values, masked):
    scores = [
        mask(lax.dot_general(q, k, (((1,), (1,)), ((), ())), preferred_element_type=F32))
        for q, k, mask in zip(queries, keys, masked)
    ]
    tops = [jnp.max(x, axis=-1, keepdims=True) for x in scores]
    expos = [jnp.exp2((x - top) * EXPONENT) for x, top in zip(scores, tops)]
    totals = [jnp.sum(x, axis=-1, keepdims=True) for x in expos]
    sums = [
        jnp.dot(x.astype(BF16), v, preferred_element_type=F32) for x, v in zip(expos, values)
    ]
    return [
        ((x * (1.0 / total)).astype(BF16), top * EXPONENT + jnp.log2(total))
        for x, top, total in zip(sums, tops, totals)
    ]


def as_row(column):
    lane = lax.broadcasted_iota(jnp.int32, (8, HD), 1)
    sublane = lax.broadcasted_iota(jnp.int32, (8, HD), 0)
    spread = jnp.zeros((8, HD), F32)
    for v in range(column.shape[0] // 8):
        spread = jnp.where(lane == sublane + 8 * v, column[8 * v : 8 * v + 8], spread)
    return jnp.sum(spread, axis=0, keepdims=True)


def kernel(
    q_hbm,
    kv_hbm,
    new_hbm,
    sel_hbm,
    w_hbm,
    out_ref,
    q_in,
    new_in,
    sel_in,
    kv,
    w,
    rows32,
    q_own,
    q_all,
    bias,
    fresh_out,
    fresh_log,
    part_out,
    part_in,
    log_out,
    log_in,
    att_own,
    att_all,
    att32,
    mix_out,
    mix_in,
    small_sem,
    kv_sem,
    w_sem,
    q_send,
    q_recv,
    part_send,
    part_recv,
    log_send,
    log_recv,
    fresh_send,
    att_send,
    att_recv,
    mix_send,
    mix_recv,
    *,
    n_ctx,
    n_head,
):
    steps = q_in.shape[0]
    pages = kv.shape[1]
    tokens = pages * PAGE
    rows = steps * GROUPS
    me = lax.axis_index("ctx")
    my_head = lax.axis_index("head")

    nx, ny, nc = axes_of(n_ctx)
    others_list = displacements(n_ctx)
    x, y, c = me // (ny * nc), (me // nc) & (ny - 1), me & (nc - 1)
    half = half_of(x, y, c, n_ctx)
    block = n_ctx // n_head
    groups = [(0, block), (block, n_ctx // 2), (n_ctx // 2, n_ctx)]
    groups = [group for group in groups if group[0] < group[1]]
    starts = [group[0] for group in groups]

    def owner(d):
        return (((x + d[0]) & (nx - 1)) * ny + ((y + d[1]) & (ny - 1))) * nc + ((c + d[2]) & (nc - 1))

    def group_of(sequence):
        return sum((sequence >= start).astype(jnp.int32) for start in starts[1:])

    def send(axis, here, to, src, dst, send_sem, recv_sem):
        @pl.when(here == to)
        def _():
            pltpu.make_async_copy(src, dst, recv_sem).start()

        @pl.when(here != to)
        def _():
            remote(axis, to, src, dst, send_sem, recv_sem).start()

    def remote(axis, to, src, dst, send_sem, recv_sem):
        return pltpu.make_async_remote_copy(
            src_ref=src,
            dst_ref=dst,
            send_sem=send_sem,
            recv_sem=recv_sem,
            device_id={axis: to},
            device_id_type=MESH,
        )

    def arrived(ref, sem):
        pltpu.make_async_copy(ref, ref, sem).wait()

    q_copy = pltpu.make_async_copy(q_hbm, q_in, small_sem.at[0])
    sel_copy = pltpu.make_async_copy(sel_hbm, sel_in, small_sem.at[1])
    new_copy = pltpu.make_async_copy(new_hbm, new_in, small_sem.at[2])
    w_copy = pltpu.make_async_copy(w_hbm, w, w_sem)
    q_copy.start()
    sel_copy.start()
    new_copy.start()

    barrier = pltpu.get_barrier_semaphore()

    for d in others_list:
        pl.semaphore_signal(barrier, inc=1, device_id={"ctx": owner(d)}, device_id_type=MESH)
    for d in by_distance(n_head):
        to = lax.rem(my_head + d, n_head)
        pl.semaphore_signal(barrier, inc=1, device_id={"head": to}, device_id_type=MESH)

    chunk = kv.shape[0] // 4
    for i in range(4):
        part = pl.ds(i * chunk, chunk)
        pltpu.make_async_copy(kv_hbm.at[part], kv.at[part], kv_sem).start()
    w_copy.start()

    q_copy.wait()
    for s in range(steps):
        for g in range(GROUPS):
            rows32[s * GROUPS + g : s * GROUPS + g + 1, :] = q_in[
                s : s + 1, g * HD : (g + 1) * HD
            ].astype(F32)
    q_own[...] = rows32[...].astype(BF16)

    pl.semaphore_wait(barrier, n_ctx - 1 + n_head - 1)

    q_sem = q_recv.at[group_of(me)]
    for d in others_list:
        remote("ctx", owner(d), q_own, q_all.at[me], q_send, q_sem).start()
    pltpu.make_async_copy(q_own, q_all.at[me], q_sem).start()

    sel_copy.wait()
    number = lax.broadcasted_iota(jnp.int32, (pages, n_ctx), 0) + me * pages
    from_b = lax.broadcasted_iota(jnp.int32, (n_ctx, n_ctx * rows), 0)
    to_lane = lax.broadcasted_iota(jnp.int32, (n_ctx, n_ctx * rows), 1)
    chosen = jnp.zeros((pages, n_ctx * rows), F32)
    for s in range(steps):
        hit = jnp.zeros((pages, n_ctx), F32)
        for j in range(sel_in.shape[1]):
            hit = jnp.where(sel_in[s, j] == number, 1.0, hit)
        spread = jnp.where(((to_lane >> log2_of(rows)) == from_b) & (((to_lane & (rows - 1)) >> 3) == s), 1.0, 0.0)
        chosen += jnp.dot(hit.astype(BF16), spread.astype(BF16), preferred_element_type=F32)
    page = lax.broadcasted_iota(jnp.int32, (pages, tokens), 0)
    token = lax.broadcasted_iota(jnp.int32, (pages, tokens), 1)
    expand = jnp.where((token >> 6) == page, 1.0, 0.0).astype(BF16)
    count = lax.dot_general(
        chosen.astype(BF16), expand, (((0,), (0,)), ((), ())), preferred_element_type=F32
    )
    bias[...] = ((count - 1.0) * -NEG).reshape(bias.shape)

    new_copy.wait()
    new_keys = jnp.concatenate(
        [new_in[:, 0].astype(F32), jnp.zeros((HD - steps, HD), F32)], axis=0
    ).astype(BF16)
    new_values = jnp.concatenate(
        [new_in[:, 1].astype(F32), jnp.zeros((HD - steps, HD), F32)], axis=0
    ).astype(BF16)
    step_of = lax.broadcasted_iota(jnp.int32, (rows, HD), 0) >> 3
    place = lax.broadcasted_iota(jnp.int32, (rows, HD), 1)

    def causal(scores):
        return jnp.where(place <= step_of, scores, NEG)

    def selected_of(b):
        def mask(scores):
            return scores + bias[b]

        return mask

    def keys_of(b):
        return kv[b, :, 0].reshape(tokens, HD)

    def values_of(b):
        return kv[b, :, 1].reshape(tokens, HD)

    own = q_own[...]
    ((normed, log),) = softmax_parts([own], [new_keys], [new_values], [causal])
    span = rows // 2
    phase = me >> log2_of(n_ctx // 2)
    fresh_to = [joiner_of((2 * me + h) & (n_ctx - 1), n_ctx) for h in range(2)]
    for h in range(2):
        fresh_out[h] = normed[h * span : (h + 1) * span]
        fresh_log[h] = as_row(log[h * span : (h + 1) * span])
    for h in range(2):
        send(
            "ctx",
            me,
            fresh_to[h],
            fresh_log.at[h],
            log_in.at[phase, n_ctx],
            fresh_send.at[h, 0],
            log_recv.at[phase],
        )
        send(
            "ctx",
            me,
            fresh_to[h],
            fresh_out.at[h],
            part_in.at[phase, n_ctx],
            fresh_send.at[h, 1],
            part_recv.at[phase],
        )
    for p in range(2):
        for i in range(n_ctx + 1, log_in.shape[1]):
            log_in[p, i] = jnp.full((1, HD), NEG, F32)
    arrived(kv, kv_sem)

    for i, (first, last) in enumerate(groups):
        arrived(q_all.at[pl.ds(0, last - first)], q_recv.at[i])
        results = softmax_parts(
            [q_all[b] for b in range(first, last)],
            [keys_of(b) for b in range(first, last)],
            [values_of(b) for b in range(first, last)],
            [selected_of(b) for b in range(first, last)],
        )
        for b, (normed, log) in zip(range(first, last), results):
            for h in range(2):
                part_out[2 * b + h] = normed[h * span : (h + 1) * span]
                log_out[2 * b + h] = as_row(log[h * span : (h + 1) * span])
        for u in range(2 * first, 2 * last):
            to, p = joiner_of(u % n_ctx, n_ctx), u // n_ctx
            send("ctx", me, to, log_out.at[u], log_in.at[p, me], log_send, log_recv.at[p])
            send("ctx", me, to, part_out.at[u], part_in.at[p, me], part_send, part_recv.at[p])

    for p in range(2):
        arrived(log_in.at[p, pl.ds(0, n_ctx + 1)], log_recv.at[p])
        logs = log_in[p].reshape(log_in.shape[1], HD)
        shares = jnp.exp2(logs - jnp.max(logs, axis=0, keepdims=True))
        shares = shares * (1.0 / jnp.sum(shares, axis=0, keepdims=True))
        columns = jnp.transpose(shares)
        arrived(part_in.at[p], part_recv.at[p])
        joined = [jnp.zeros((8, HD), F32) for _ in range(span // 8)]
        for i in range(n_ctx + 1):
            part = part_in[p, i].astype(F32)
            for v in range(span // 8):
                joined[v] += part[8 * v : 8 * v + 8] * columns[8 * v : 8 * v + 8, i : i + 1]
        att_own[p] = jnp.concatenate(joined, axis=0).astype(BF16)
        place = half + p * n_ctx
        att_sem = att_recv.at[group_of(place >> 1)]
        for d in others_list:
            remote("ctx", owner(d), att_own.at[p], att_all.at[place], att_send, att_sem).start()
        pltpu.make_async_copy(att_own.at[p], att_all.at[place], att_sem).start()

    w_copy.wait()
    for i, (first, last) in enumerate(groups):
        units = pl.ds(2 * first, 2 * (last - first))
        arrived(att_all.at[units], att_recv.at[i])
        base, count = first * rows, (last - first) * steps
        att32[base : base + count * GROUPS, :] = (
            att_all[2 * first : 2 * last].astype(F32).reshape(count * GROUPS, HD)
        )
        flat = jnp.concatenate(
            [att32[pl.ds(base + g, count, stride=GROUPS), :].astype(BF16) for g in range(GROUPS)],
            axis=1,
        )
        mixed = jnp.dot(flat, w[...], preferred_element_type=F32).astype(BF16)
        for to in range(first // block, last // block):
            row = (to * block - first) * steps
            mix_out[to] = mixed[row : row + block * steps]
        for to in range(first // block, last // block):
            send("head", my_head, to, mix_out.at[to], mix_in.at[my_head], mix_send, mix_recv)

    arrived(q_all.at[pl.ds(0, n_ctx - 1)], q_send)
    arrived(part_out.at[pl.ds(0, 2 * n_ctx - 2)], part_send)
    arrived(log_out.at[pl.ds(0, 2 * n_ctx - 2)], log_send)
    arrived(att_all.at[pl.ds(0, 2 * n_ctx - 2)], att_send)
    for h in range(2):

        @pl.when(me != fresh_to[h])
        def _():
            arrived(fresh_log.at[h], fresh_send.at[h, 0])
            arrived(fresh_out.at[h], fresh_send.at[h, 1])

    arrived(mix_in, mix_recv)
    out_ref[...] = jnp.sum(mix_in[...].astype(F32), axis=0).astype(BF16)
    arrived(mix_out.at[pl.ds(0, n_head - 1)], mix_send)


def local(queries, kv_cache, new_kv, selected, out_weight, *, n_ctx, n_head):
    steps, _, width = queries.shape
    batch, pages = kv_cache.shape[:2]
    rows = steps * GROUPS
    columns = out_weight.shape[1]
    own = batch // n_head * steps
    dma = pltpu.SemaphoreType.DMA
    any_space = pl.BlockSpec(memory_space=pl.ANY)
    sel = jnp.transpose(selected, (0, 3, 2, 1))
    result = pl.pallas_call(
        functools.partial(kernel, n_ctx=n_ctx, n_head=n_head),
        out_shape=jax.ShapeDtypeStruct((own, columns), BF16),
        in_specs=[any_space] * 5,
        out_specs=pl.BlockSpec(memory_space=pltpu.VMEM),
        scratch_shapes=[
            pltpu.VMEM((steps, width), BF16),
            pltpu.VMEM((steps, 2, HD), BF16),
            pltpu.VMEM(sel.shape, jnp.int32),
            pltpu.VMEM(kv_cache.shape, BF16),
            pltpu.VMEM(out_weight.shape, BF16),
            pltpu.VMEM((rows, HD), F32),
            pltpu.VMEM((rows, HD), BF16),
            pltpu.VMEM((batch, rows, HD), BF16),
            pltpu.VMEM((batch, rows, pages * PAGE), F32),
            pltpu.VMEM((2, rows // 2, HD), BF16),
            pltpu.VMEM((2, 1, HD), F32),
            pltpu.VMEM((2 * batch, rows // 2, HD), BF16),
            pltpu.VMEM((2, n_ctx + 1, rows // 2, HD), BF16),
            pltpu.VMEM((2 * batch, 1, HD), F32),
            pltpu.VMEM((2, n_ctx + 8, 1, HD), F32),
            pltpu.VMEM((2, rows // 2, HD), BF16),
            pltpu.VMEM((2 * batch, rows // 2, HD), BF16),
            pltpu.VMEM((batch * rows, HD), F32),
            pltpu.VMEM((n_head, own, columns), BF16),
            pltpu.VMEM((n_head, own, columns), BF16),
            dma((3,)),
            dma,
            dma,
            dma,
            dma((3,)),
            dma,
            dma((2,)),
            dma,
            dma((2,)),
            dma((2, 2)),
            dma,
            dma((3,)),
            dma,
            dma,
        ],
        compiler_params=pltpu.CompilerParams(
            collective_id=0, has_side_effects=True, vmem_limit_bytes=56 * 1024 * 1024
        ),
    )(
        queries.reshape(steps, width),
        kv_cache,
        new_kv.reshape(steps, 2, HD),
        sel,
        out_weight,
    )
    return result.reshape(batch // n_head, steps, columns)


def solution(mesh):
    n_ctx, n_head = mesh.shape["ctx"], mesh.shape["head"]
    return jax.shard_map(
        functools.partial(local, n_ctx=n_ctx, n_head=n_head),
        mesh=mesh,
        in_specs=(
            P(None, "ctx", "head"),
            P(None, "ctx", None, None, "head"),
            P(None, "ctx", None, "head"),
            P(None, None, "head", None),
            P("head", "ctx"),
        ),
        out_specs=P("head", None, "ctx"),
        check_vma=False,
    )
```

time: 35.1 us -> 32.8 us (0.934)
  Pallas kernels: 33.6 us -> 31 us
    pallas_call x1, Pallas kernels: 33.6 us -> 31 us  [local(): pl.pallas_call(functools.partial(kernel, n_ctx=n_ctx, n_head=n_head), out...]
where the time goes in v3:
time: 32.8 us; the launch traced here: 32.3 us
  Pallas kernels  31 us (95%)
  local copies, waits for them, and re-layouts  1.3 us (4%)
    pallas_call x1, Pallas kernels, local(): pl.pallas_call(functools.partial(kernel, n_ctx=n_ctx, n_head=n_head), out...  31 us
    reshape x1, local copies, waits for them, and re-layouts, local(): return result.reshape(batch // n_head, steps, columns)  1.3 us

profile of v3, /device:TPU:1, one launch (start us, length us, event | category | flops | bytes accessed | tf_op | source)
XLA Modules:
  0.0 32.3 jit_solution(7183298939090524076)
XLA Ops:
  0.0 31.0 %shard_map.55 = bf16[16,256]{1,0:T(8,128)(2,1)} custom-call(bf16[4,1024]{1,0:T(4,128)(2,1)} %bitcast.4, bf16[32,8,2,64,128]{4,3,2,1,0:T(8,128)(2,1)} %kv_hbm.1, bf16[4,2,128]{2,1,0:T(2,128)(2,1)} %bitcast.5, s32[4,20,1,32]{3,2,1,0:T(1,128)} %bitcast.3, bf16[1024,256]{1,0:T(8,128)(2,1)} %w_hbm.1), custom_call_target="tpu_custom_call" | custom-call | tf_op jit(solution)/shard_map/pallas_call | solution.py:365
  31.0 1.3 %reshape.11 = bf16[4,4,256]{2,1,0:T(4,128)(2,1)} reshape(bf16[16,256]{1,0:T(8,128)(2,1)} %shard_map.55) | data formatting | bytes 16384 | tf_op jit(solution)/shard_map/reshape | solution.py:416

commit v4 on v3

--- a/solution.py
+++ b/solution.py
@@ -106,7 +106,6 @@
     att_all,
     att32,
     mix_out,
-    mix_in,
     small_sem,
     kv_sem,
     w_sem,
@@ -137,8 +136,8 @@
     x, y, c = me // (ny * nc), (me // nc) & (ny - 1), me & (nc - 1)
     half = half_of(x, y, c, n_ctx)
     block = n_ctx // n_head
-    groups = [(0, block), (block, n_ctx // 2), (n_ctx // 2, n_ctx)]
-    groups = [group for group in groups if group[0] < group[1]]
+    bounds = sorted({0, block, 2 * block, n_ctx // 2, n_ctx})
+    groups = list(zip(bounds, bounds[1:]))
     starts = [group[0] for group in groups]
 
     def owner(d):
@@ -335,7 +334,7 @@
             row = (to * block - first) * steps
             mix_out[to] = mixed[row : row + block * steps]
         for to in range(first // block, last // block):
-            send("head", my_head, to, mix_out.at[to], mix_in.at[my_head], mix_send, mix_recv)
+            send("head", my_head, to, mix_out.at[to], out_ref.at[my_head], mix_send, mix_recv)
 
     arrived(q_all.at[pl.ds(0, n_ctx - 1)], q_send)
     arrived(part_out.at[pl.ds(0, 2 * n_ctx - 2)], part_send)
@@ -348,9 +347,8 @@
             arrived(fresh_log.at[h], fresh_send.at[h, 0])
             arrived(fresh_out.at[h], fresh_send.at[h, 1])
 
-    arrived(mix_in, mix_recv)
-    out_ref[...] = jnp.sum(mix_in[...].astype(F32), axis=0).astype(BF16)
     arrived(mix_out.at[pl.ds(0, n_head - 1)], mix_send)
+    arrived(out_ref, mix_recv)
 
 
 def local(queries, kv_cache, new_kv, selected, out_weight, *, n_ctx, n_head):
@@ -364,9 +362,9 @@
     sel = jnp.transpose(selected, (0, 3, 2, 1))
     result = pl.pallas_call(
         functools.partial(kernel, n_ctx=n_ctx, n_head=n_head),
-        out_shape=jax.ShapeDtypeStruct((own, columns), BF16),
+        out_shape=jax.ShapeDtypeStruct((n_head, own, columns), BF16),
         in_specs=[any_space] * 5,
-        out_specs=pl.BlockSpec(memory_space=pltpu.VMEM),
+        out_specs=any_space,
         scratch_shapes=[
             pltpu.VMEM((steps, width), BF16),
             pltpu.VMEM((steps, 2, HD), BF16),
@@ -387,19 +385,18 @@
             pltpu.VMEM((2 * batch, rows // 2, HD), BF16),
             pltpu.VMEM((batch * rows, HD), F32),
             pltpu.VMEM((n_head, own, columns), BF16),
-            pltpu.VMEM((n_head, own, columns), BF16),
             dma((3,)),
             dma,
             dma,
             dma,
-            dma((3,)),
+            dma((4,)),
             dma,
             dma((2,)),
             dma,
             dma((2,)),
             dma((2, 2)),
             dma,
-            dma((3,)),
+            dma((4,)),
             dma,
             dma,
         ],
@@ -413,6 +410,7 @@
         sel,
         out_weight,
     )
+    result = jnp.sum(result.astype(F32), axis=0).astype(BF16)
     return result.reshape(batch // n_head, steps, columns)
 
 

time: 32.8 us -> 32.1 us (0.979); the launches traced: 32.3 us -> 32 us
  other arithmetic: 0 us -> 0.86 us
  local copies, waits for them, and re-layouts: 1.3 us -> 0.61 us
  Pallas kernels: 31 us -> 30.5 us
    reduce_sum x0 -> x1, other arithmetic: none -> 0.86 us  [local(): result = jnp.sum(result.astype(F32), axis=0).astype(BF16)]
    reshape x1, local copies, waits for them, and re-layouts: 1.3 us -> 0.61 us  [local(): return result.reshape(batch // n_head, steps, columns)]
    pallas_call x1, Pallas kernels: 31 us -> 30.5 us  [local(): pl.pallas_call(functools.partial(kernel, n_ctx=n_ctx, n_head=n_head), out...]
where the time goes in v4:
time: 32.1 us; the launch traced here: 32 us
  Pallas kernels  30.5 us (95%)
  other arithmetic  0.86 us (3%)
  local copies, waits for them, and re-layouts  0.61 us (2%)
    pallas_call x1, Pallas kernels, local(): pl.pallas_call(functools.partial(kernel, n_ctx=n_ctx, n_head=n_head), out...  30.5 us
    reduce_sum x1, other arithmetic, local(): result = jnp.sum(result.astype(F32), axis=0).astype(BF16)  0.86 us

profile of v4, /device:TPU:1, one launch (start us, length us, event | category | flops | bytes accessed | tf_op | source)
XLA Modules:
  0.0 32.0 jit_solution(7372336633688944864)
XLA Ops:
  0.0 30.5 %shard_map.55 = bf16[8,16,256]{2,1,0:T(8,128)(2,1)} custom-call(bf16[4,1024]{1,0:T(4,128)(2,1)} %bitcast.4, bf16[32,8,2,64,128]{4,3,2,1,0:T(8,128)(2,1)} %kv_hbm.1, bf16[4,2,128]{2,1,0:T(2,128)(2,1)} %bitcast.5, s32[4,20,1,32]{3,2,1,0:T(1,128)} %bitcast.3, bf16[1024,256]{1,0:T(8,128)(2,1)} %w_hbm.1), custom_call_target="tpu_custom_call" | custom-call | tf_op jit(solution)/shard_map/pallas_call | solution.py:363
  30.5 0.9 %reduce_sum.12 = bf16[16,256]{1,0:T(8,128)(2,1)S(1)} reduce(bf16[8,16,256]{2,1,0:T(8,128)(2,1)} %shard_map.55, bf16[]{:T(256)} %constant.2.clone.1), dimensions={0}, to_apply=%region_0.0 | reduce | flops 28672 | bytes 73730 | tf_op jit(solution)/shard_map/reduce_sum | solution.py:413
  31.4 0.6 %reshape.11 = bf16[4,4,256]{2,1,0:T(4,128)(2,1)} reshape(bf16[16,256]{1,0:T(8,128)(2,1)S(1)} %reduce_sum.12) | data formatting | bytes 16384 | tf_op jit(solution)/shard_map/reshape | solution.py:414

commit v5 on v4

--- a/solution.py
+++ b/solution.py
@@ -106,6 +106,7 @@
     att_all,
     att32,
     mix_out,
+    mix_in,
     small_sem,
     kv_sem,
     w_sem,
@@ -334,7 +335,7 @@
             row = (to * block - first) * steps
             mix_out[to] = mixed[row : row + block * steps]
         for to in range(first // block, last // block):
-            send("head", my_head, to, mix_out.at[to], out_ref.at[my_head], mix_send, mix_recv)
+            send("head", my_head, to, mix_out.at[to], mix_in.at[my_head], mix_send, mix_recv)
 
     arrived(q_all.at[pl.ds(0, n_ctx - 1)], q_send)
     arrived(part_out.at[pl.ds(0, 2 * n_ctx - 2)], part_send)
@@ -348,7 +349,10 @@
             arrived(fresh_out.at[h], fresh_send.at[h, 1])
 
     arrived(mix_out.at[pl.ds(0, n_head - 1)], mix_send)
-    arrived(out_ref, mix_recv)
+    arrived(mix_in, mix_recv)
+    total = jnp.sum(mix_in[...].astype(F32), axis=0)
+    for i in range(out_ref.shape[0]):
+        out_ref[i] = total[i * steps : (i + 1) * steps].astype(BF16)
 
 
 def local(queries, kv_cache, new_kv, selected, out_weight, *, n_ctx, n_head):
@@ -362,9 +366,9 @@
     sel = jnp.transpose(selected, (0, 3, 2, 1))
     result = pl.pallas_call(
         functools.partial(kernel, n_ctx=n_ctx, n_head=n_head),
-        out_shape=jax.ShapeDtypeStruct((n_head, own, columns), BF16),
+        out_shape=pltpu.VMEM((own // steps, steps, columns), BF16),
         in_specs=[any_space] * 5,
-        out_specs=any_space,
+        out_specs=pl.BlockSpec(memory_space=pltpu.VMEM),
         scratch_shapes=[
             pltpu.VMEM((steps, width), BF16),
             pltpu.VMEM((steps, 2, HD), BF16),
@@ -385,6 +389,7 @@
             pltpu.VMEM((2 * batch, rows // 2, HD), BF16),
             pltpu.VMEM((batch * rows, HD), F32),
             pltpu.VMEM((n_head, own, columns), BF16),
+            pltpu.VMEM((n_head, own, columns), BF16),
             dma((3,)),
             dma,
             dma,
@@ -410,8 +415,7 @@
         sel,
         out_weight,
     )
-    result = jnp.sum(result.astype(F32), axis=0).astype(BF16)
-    return result.reshape(batch // n_head, steps, columns)
+    return result
 
 
 def solution(mesh):

time: 32.1 us -> 31.2 us (0.972)
  other arithmetic: 0.86 us -> 0 us
    reduce_sum x1 -> x0, other arithmetic: 0.86 us -> none  [local(): result = jnp.sum(result.astype(F32), axis=0).astype(BF16)]
    reshape x1 -> x0, local copies, waits for them, and re-layouts: 0.61 us -> none  [local(): return result.reshape(batch // n_head, steps, columns)]
    unnamed x0 -> x1, local copies, waits for them, and re-layouts: none -> 0.6 us
where the time goes in v5:
time: 31.2 us; the launch traced here: 31.1 us
  Pallas kernels  30.4 us (97%)
  local copies, waits for them, and re-layouts  0.6 us (2%)
    pallas_call x1, Pallas kernels, local(): pl.pallas_call(functools.partial(kernel, n_ctx=n_ctx, n_head=n_head), out...  30.4 us

profile of v5, /device:TPU:1, one launch (start us, length us, event | category | flops | bytes accessed | tf_op | source)
XLA Modules:
  0.0 31.1 jit_solution(4644603952977636565)
XLA Ops:
  0.0 30.4 %shard_map.55 = bf16[4,4,256]{2,1,0:T(4,128)(2,1)S(1)} custom-call(bf16[4,1024]{1,0:T(4,128)(2,1)} %bitcast.4, bf16[32,8,2,64,128]{4,3,2,1,0:T(8,128)(2,1)} %kv_hbm.1, bf16[4,2,128]{2,1,0:T(2,128)(2,1)} %bitcast.5, s32[4,20,1,32]{3,2,1,0:T(1,128)} %bitcast.3, bf16[1024,256]{1,0:T(8,128)(2,1)} %w_hbm.1), custom_call_target="tpu_custom_call" | custom-call | tf_op jit(solution)/shard_map/pallas_call | solution.py:367
  30.5 0.6 %copy.7 = bf16[4,4,256]{2,1,0:T(4,128)(2,1)} copy(bf16[4,4,256]{2,1,0:T(4,128)(2,1)S(1)} %shard_map.55) | data formatting | bytes 16384

commit v6 on v5

--- a/solution.py
+++ b/solution.py
@@ -303,15 +303,14 @@
         arrived(log_in.at[p, pl.ds(0, n_ctx + 1)], log_recv.at[p])
         logs = log_in[p].reshape(log_in.shape[1], HD)
         shares = jnp.exp2(logs - jnp.max(logs, axis=0, keepdims=True))
-        shares = shares * (1.0 / jnp.sum(shares, axis=0, keepdims=True))
-        columns = jnp.transpose(shares)
+        columns = jnp.transpose(shares)[0:span]
+        inverse = 1.0 / jnp.sum(columns, axis=1, keepdims=True)
         arrived(part_in.at[p], part_recv.at[p])
-        joined = [jnp.zeros((8, HD), F32) for _ in range(span // 8)]
+        chains = [jnp.zeros((span, HD), F32) for _ in range(4)]
         for i in range(n_ctx + 1):
-            part = part_in[p, i].astype(F32)
-            for v in range(span // 8):
-                joined[v] += part[8 * v : 8 * v + 8] * columns[8 * v : 8 * v + 8, i : i + 1]
-        att_own[p] = jnp.concatenate(joined, axis=0).astype(BF16)
+            chains[i % 4] += part_in[p, i].astype(F32) * columns[:, i : i + 1]
+        joined = (chains[0] + chains[1]) + (chains[2] + chains[3])
+        att_own[p] = (joined * inverse).astype(BF16)
         place = half + p * n_ctx
         att_sem = att_recv.at[group_of(place >> 1)]
         for d in others_list:

time: 31.2 us -> 31.2 us (level)
  no operation moved by 1% of the time
where the time goes in v6:
time: 31.2 us; the launch traced here: 31.1 us
  Pallas kernels  30.5 us (98%)
  local copies, waits for them, and re-layouts  0.6 us (2%)
    pallas_call x1, Pallas kernels, local(): pl.pallas_call(functools.partial(kernel, n_ctx=n_ctx, n_head=n_head), out...  30.5 us

profile of v6, /device:TPU:1, one launch (start us, length us, event | category | flops | bytes accessed | tf_op | source)
XLA Modules:
  0.0 31.1 jit_solution(6667304367840497706)
XLA Ops:
  0.0 30.5 %shard_map.55 = bf16[4,4,256]{2,1,0:T(4,128)(2,1)S(1)} custom-call(bf16[4,1024]{1,0:T(4,128)(2,1)} %bitcast.4, bf16[32,8,2,64,128]{4,3,2,1,0:T(8,128)(2,1)} %kv_hbm.1, bf16[4,2,128]{2,1,0:T(2,128)(2,1)} %bitcast.5, s32[4,20,1,32]{3,2,1,0:T(1,128)} %bitcast.3, bf16[1024,256]{1,0:T(8,128)(2,1)} %w_hbm.1), custom_call_target="tpu_custom_call" | custom-call | tf_op jit(solution)/shard_map/pallas_call | solution.py:366
  30.5 0.6 %copy.7 = bf16[4,4,256]{2,1,0:T(4,128)(2,1)} copy(bf16[4,4,256]{2,1,0:T(4,128)(2,1)S(1)} %shard_map.55) | data formatting | bytes 16384

commit v7 on v6

--- a/solution.py
+++ b/solution.py
@@ -33,7 +33,7 @@
 
 def half_of(x, y, c, size):
     nx, ny, _ = axes_of(size)
-    return c * (nx * ny) + ((x + y) & 1) * (nx * ny // 2) + x * (ny // 2) + (y >> 1)
+    return c * (nx * ny) + x * ny + y
 
 
 def log2_of(size):
@@ -42,11 +42,8 @@
 
 def joiner_of(half, size):
     nx, ny, nc = axes_of(size)
-    chips = nx * ny
-    c, place = half >> log2_of(chips), half & (chips - 1)
-    odd, place = place >> log2_of(chips // 2), place & (chips // 2 - 1)
-    x = place >> log2_of(ny // 2)
-    y = 2 * (place & (ny // 2 - 1)) + ((x + odd) & 1)
+    c, place = half >> log2_of(nx * ny), half & (nx * ny - 1)
+    x, y = place >> log2_of(ny), place & (ny - 1)
     return (x * ny + y) * nc + c
 
 

time: 31.2 us -> 31.2 us (level)
  no operation moved by 1% of the time
where the time goes in v7:
time: 31.2 us; the launch traced here: 30.9 us
  Pallas kernels  30.3 us (97%)
  local copies, waits for them, and re-layouts  0.6 us (2%)
    pallas_call x1, Pallas kernels, local(): pl.pallas_call(functools.partial(kernel, n_ctx=n_ctx, n_head=n_head), out...  30.3 us

profile of v7, /device:TPU:1, one launch (start us, length us, event | category | flops | bytes accessed | tf_op | source)
XLA Modules:
  0.0 30.9 jit_solution(9895694562896114486)
XLA Ops:
  0.0 30.3 %shard_map.55 = bf16[4,4,256]{2,1,0:T(4,128)(2,1)S(1)} custom-call(bf16[4,1024]{1,0:T(4,128)(2,1)} %bitcast.4, bf16[32,8,2,64,128]{4,3,2,1,0:T(8,128)(2,1)} %kv_hbm.1, bf16[4,2,128]{2,1,0:T(2,128)(2,1)} %bitcast.5, s32[4,20,1,32]{3,2,1,0:T(1,128)} %bitcast.3, bf16[1024,256]{1,0:T(8,128)(2,1)} %w_hbm.1), custom_call_target="tpu_custom_call" | custom-call | tf_op jit(solution)/shard_map/pallas_call | solution.py:363
  30.3 0.6 %copy.7 = bf16[4,4,256]{2,1,0:T(4,128)(2,1)} copy(bf16[4,4,256]{2,1,0:T(4,128)(2,1)S(1)} %shard_map.55) | data formatting | bytes 16384
